TPU v7x, 512 devices: a whole 4x8x8 slice. The times are simulated.
512 devices in a mesh: blk: 64 (over z, y_lo, x), layer: 8 (over y_hi, core).
Axes of the slice: x: 4, y: 8 (y_hi: 4, y_lo: 2; y = y_hi * 2 + y_lo), z: 8, core: 2. Of those that a mesh axis runs over, the one named last changes fastest.
Arguments:
- points: bfloat16 [65536, 128], P('blk'), may hold values from -12 to 12, as said below
- directions: bfloat16 [65536, 64], P('blk'), may hold values from -0.09375 to 0.09375
Outputs:
- product: float32 [65536, 64], P(('blk', 'layer'))
Inputs may be any that keep to these rules, and one draw needn't show every extreme that they name: `points`: embeddings with row scales that differ from row to row.
All inputs are finite; a program needn't handle non-finite values.
Results may differ from a plain program's by a relative error of at most 0.0033.
Values may be sent and summed in bfloat16 or wider, within the bound.
A program may use at most 64 MiB of HBM per device.

v0:
```python
import jax
import jax.numpy as jnp
from jax import lax
from jax.sharding import PartitionSpec as P


def shifted(array, axis, by):
    count = lax.axis_size(axis)
    return lax.ppermute(array, axis, [(i, (i + by) % count) for i in range(count)])


def local(points, directions):
    layers = lax.axis_size("layer")
    blocks = lax.axis_size("blk")
    span = blocks // layers
    layer_id = lax.axis_index("layer")
    rows = points.shape[0]
    feats = points.shape[1]
    gamma = 0.5 / feats
    wide = points.astype(jnp.float32)
    own_norms = jnp.sum(wide * wide, axis=1)
    packed = jnp.concatenate([points, directions], axis=1)
    for bit in range(layers.bit_length() - 1):
        moved = shifted(packed, "blk", span << bit)
        packed = jnp.where(layer_id >> bit & 1 == 1, moved, packed)
    total = jnp.zeros((rows, directions.shape[1]), jnp.float32)
    for step in range(span):
        source = packed[:, :feats]
        weights = packed[:, feats:]
        wide_src = source.astype(jnp.float32)
        src_norms = jnp.sum(wide_src * wide_src, axis=1)
        gram = lax.dot_general(
            points, source, (((1,), (1,)), ((), ())), preferred_element_type=jnp.float32
        )
        dist = jnp.maximum(own_norms[:, None] + src_norms[None, :] - 2.0 * gram, 0.0)
        kernel = jnp.exp(-gamma * dist).astype(jnp.bfloat16)
        total = total + jnp.dot(kernel, weights, preferred_element_type=jnp.float32)
        if step + 1 < span:
            packed = shifted(packed, "blk", 1)
    share = rows // layers
    summed = lax.psum(total, "layer")
    mine = lax.dynamic_slice_in_dim(summed, layer_id * share, share, 0)
    return mine


def solution(mesh):
    in_specs = (P("blk", None), P("blk", None))
    out_specs = P(("blk", "layer"), None)
    return jax.shard_map(local, mesh=mesh, in_specs=in_specs, out_specs=out_specs, check_vma=False)
```

profile of v0, /device:TPU:1, one launch (start us, length us, event | category | flops | bytes accessed | tf_op | source)
XLA Modules:
  0.0 300.3 jit_solution(6301751453999741529)
XLA Ops:
  7.8 4.8 %collective-permute-start = (bf16[1024,192]{1,0:T(8,128)(2,1)S(1)}, bf16[1024,192]{1,0:T(8,128)(2,1)S(1)}, u32[]{:S(2)}, u32[]{:S(2)}) collective-permute-start(bf16[1024,192]{1,0:T(8,128)(2,1)S(1)} %pad_maximum_fusion), channel_id=1, source_target_pairs={{0,64},{8,72},{16,80},{24,88},{32,96},{40,104},{48,112},{56,120},{... | collective-permute-start | bytes 1179656 | tf_op jit(solution)/shard_map/ppermute | solution.py:9
  12.6 18.3 %collective-permute-done = bf16[1024,192]{1,0:T(8,128)(2,1)S(1)} collective-permute-done((bf16[1024,192]{1,0:T(8,128)(2,1)S(1)}, bf16[1024,192]{1,0:T(8,128)(2,1)S(1)}, u32[]{:S(2)}, u32[]{:S(2)}) %collective-permute-start) | collective-permute-done | bytes 393248 | tf_op jit(solution)/shard_map/ppermute | solution.py:9
  31.1 1.9 collective-permute-start.1
  33.0 25.5 %collective-permute-done.1 = bf16[1024,192]{1,0:T(8,128)(2,1)S(1)} collective-permute-done((bf16[1024,192]{1,0:T(8,128)(2,1)S(1)}, bf16[1024,192]{1,0:T(8,128)(2,1)S(1)}, u32[]{:S(2)}, u32[]{:S(2)}) %collective-permute-start.1) | collective-permute-done | bytes 393248 | tf_op jit(solution)/shard_map/ppermute | solution.py:9
  58.6 3.5 %collective-permute-start.2 = (bf16[1024,192]{1,0:T(8,128)(2,1)S(1)}, bf16[1024,192]{1,0:T(8,128)(2,1)S(1)}, u32[]{:S(2)}, u32[]{:S(2)}) collective-permute-start(bf16[1024,192]{1,0:T(8,128)(2,1)S(1)} %broadcast_select_fusion.1), channel_id=1, source_target_pairs={{0,256},{8,264},{16,272},{24,280},{32,288},{40,296},{48,304},{56,3... | collective-permute-start | bytes 1179656 | tf_op jit(solution)/shard_map/ppermute | solution.py:9
  62.1 25.8 %collective-permute-done.2 = bf16[1024,192]{1,0:T(8,128)(2,1)S(1)} collective-permute-done((bf16[1024,192]{1,0:T(8,128)(2,1)S(1)}, bf16[1024,192]{1,0:T(8,128)(2,1)S(1)}, u32[]{:S(2)}, u32[]{:S(2)}) %collective-permute-start.2) | collective-permute-done | bytes 393248 | tf_op jit(solution)/shard_map/ppermute | solution.py:9
  88.0 3.1 %collective-permute-start.3 = (bf16[1024,192]{1,0:T(8,128)(2,1)S(1)}, bf16[1024,192]{1,0:T(8,128)(2,1)S(1)}, u32[]{:S(2)}, u32[]{:S(2)}) collective-permute-start(bf16[1024,192]{1,0:T(8,128)(2,1)S(1)} %broadcast_select_fusion.2), channel_id=1, source_target_pairs={{0,8},{8,16},{16,24},{24,32},{32,40},{40,48},{48,56},{56,64},{64,7... | collective-permute-start | bytes 1179656 | tf_op jit(solution)/shard_map/ppermute | solution.py:9
  91.6 14.6 %collective-permute-done.3 = bf16[1024,192]{1,0:T(8,128)(2,1)S(1)} collective-permute-done((bf16[1024,192]{1,0:T(8,128)(2,1)S(1)}, bf16[1024,192]{1,0:T(8,128)(2,1)S(1)}, u32[]{:S(2)}, u32[]{:S(2)}) %collective-permute-start.3) | collective-permute-done | bytes 393248 | tf_op jit(solution)/shard_map/ppermute | solution.py:9
  106.4 1.9 collective-permute-start.4
  108.3 1.7 fusion.33
  111.7 11.7 %collective-permute-done.4 = bf16[1024,192]{1,0:T(8,128)(2,1)S(1)} collective-permute-done((bf16[1024,192]{1,0:T(8,128)(2,1)S(1)}, bf16[1024,192]{1,0:T(8,128)(2,1)S(1)}, u32[]{:S(2)}, u32[]{:S(2)}) %collective-permute-start.4) | collective-permute-done | bytes 393248 | tf_op jit(solution)/shard_map/ppermute | solution.py:9
  123.4 1.9 collective-permute-start.5
  125.6 1.7 fusion.45
  127.2 12.3 %collective-permute-done.5 = bf16[1024,192]{1,0:T(8,128)(2,1)S(1)} collective-permute-done((bf16[1024,192]{1,0:T(8,128)(2,1)S(1)}, bf16[1024,192]{1,0:T(8,128)(2,1)S(1)}, u32[]{:S(2)}, u32[]{:S(2)}) %collective-permute-start.5) | collective-permute-done | bytes 393248 | tf_op jit(solution)/shard_map/ppermute | solution.py:9
  139.5 1.9 collective-permute-start.6
  143.3 11.3 %collective-permute-done.6 = bf16[1024,192]{1,0:T(8,128)(2,1)S(1)} collective-permute-done((bf16[1024,192]{1,0:T(8,128)(2,1)S(1)}, bf16[1024,192]{1,0:T(8,128)(2,1)S(1)}, u32[]{:S(2)}, u32[]{:S(2)}) %collective-permute-start.6) | collective-permute-done | bytes 393248 | tf_op jit(solution)/shard_map/ppermute | solution.py:9
  154.7 1.9 collective-permute-start.7
  158.5 10.3 %collective-permute-done.7 = bf16[1024,192]{1,0:T(8,128)(2,1)S(1)} collective-permute-done((bf16[1024,192]{1,0:T(8,128)(2,1)S(1)}, bf16[1024,192]{1,0:T(8,128)(2,1)S(1)}, u32[]{:S(2)}, u32[]{:S(2)}) %collective-permute-start.7) | collective-permute-done | bytes 393248 | tf_op jit(solution)/shard_map/ppermute | solution.py:9
  168.8 2.1 collective-permute-start.8
  172.8 10.1 %collective-permute-done.8 = bf16[1024,192]{1,0:T(8,128)(2,1)S(1)} collective-permute-done((bf16[1024,192]{1,0:T(8,128)(2,1)S(1)}, bf16[1024,192]{1,0:T(8,128)(2,1)S(1)}, u32[]{:S(2)}, u32[]{:S(2)}) %collective-permute-start.8) | collective-permute-done | bytes 393248 | tf_op jit(solution)/shard_map/ppermute | solution.py:9
  182.9 1.9 collective-permute-start.9
  186.7 10.3 %collective-permute-done.9 = bf16[1024,192]{1,0:T(8,128)(2,1)S(1)} collective-permute-done((bf16[1024,192]{1,0:T(8,128)(2,1)S(1)}, bf16[1024,192]{1,0:T(8,128)(2,1)S(1)}, u32[]{:S(2)}, u32[]{:S(2)}) %collective-permute-start.9) | collective-permute-done | bytes 393248 | tf_op jit(solution)/shard_map/ppermute | solution.py:9
  197.3 2.4 fusion.40
  199.7 92.4 %all-reduce.2.cloned.1.call-done = f32[1024,64]{0,1:T(8,128)} async-done(((f32[1024,64]{0,1:T(8,128)}), f32[1024,64]{0,1:T(8,128)}) %all-reduce.2.cloned.1.call-update) | async-done | bytes 262160 | tf_op jit(solution)/shard_map/psum | solution.py:41
  (24 shorter events, 13.1 us)
Async XLA Ops:
  6.5 1.1 copy-start
  6.5 285.6 %all-reduce.2.cloned.1.call-start = ((), (), s32[]{:S(2)}) async-start(), calls=%async_computation | async-start | bytes 524288 | tf_op jit(solution)/shard_map/psum | solution.py:41
  7.8 23.1 %collective-permute-start = (bf16[1024,192]{1,0:T(8,128)(2,1)S(1)}, bf16[1024,192]{1,0:T(8,128)(2,1)S(1)}, u32[]{:S(2)}, u32[]{:S(2)}) collective-permute-start(bf16[1024,192]{1,0:T(8,128)(2,1)S(1)} %pad_maximum_fusion), channel_id=1, source_target_pairs={{0,64},{8,72},{16,80},{24,88},{32,96},{40,104},{48,112},{56,120},{... | collective-permute-start | bytes 1179656 | tf_op jit(solution)/shard_map/ppermute | solution.py:9
  31.1 27.5 %collective-permute-start.1 = (bf16[1024,192]{1,0:T(8,128)(2,1)S(1)}, bf16[1024,192]{1,0:T(8,128)(2,1)S(1)}, u32[]{:S(2)}, u32[]{:S(2)}) collective-permute-start(bf16[1024,192]{1,0:T(8,128)(2,1)S(1)} %broadcast_select_fusion), channel_id=1, source_target_pairs={{0,128},{8,136},{16,144},{24,152},{32,160},{40,168},{48,176},{56,1... | collective-permute-start | bytes 1179656 | tf_op jit(solution)/shard_map/ppermute | solution.py:9
  58.6 29.3 %collective-permute-start.2 = (bf16[1024,192]{1,0:T(8,128)(2,1)S(1)}, bf16[1024,192]{1,0:T(8,128)(2,1)S(1)}, u32[]{:S(2)}, u32[]{:S(2)}) collective-permute-start(bf16[1024,192]{1,0:T(8,128)(2,1)S(1)} %broadcast_select_fusion.1), channel_id=1, source_target_pairs={{0,256},{8,264},{16,272},{24,280},{32,288},{40,296},{48,304},{56,3... | collective-permute-start | bytes 1179656 | tf_op jit(solution)/shard_map/ppermute | solution.py:9
  88.0 18.2 %collective-permute-start.3 = (bf16[1024,192]{1,0:T(8,128)(2,1)S(1)}, bf16[1024,192]{1,0:T(8,128)(2,1)S(1)}, u32[]{:S(2)}, u32[]{:S(2)}) collective-permute-start(bf16[1024,192]{1,0:T(8,128)(2,1)S(1)} %broadcast_select_fusion.2), channel_id=1, source_target_pairs={{0,8},{8,16},{16,24},{24,32},{32,40},{40,48},{48,56},{56,64},{64,7... | collective-permute-start | bytes 1179656 | tf_op jit(solution)/shard_map/ppermute | solution.py:9
  106.4 17.0 %collective-permute-start.4 = (bf16[1024,192]{1,0:T(8,128)(2,1)S(1)}, bf16[1024,192]{1,0:T(8,128)(2,1)S(1)}, u32[]{:S(2)}, u32[]{:S(2)}) collective-permute-start(bf16[1024,192]{1,0:T(8,128)(2,1)S(1)} %collective-permute-done.3), channel_id=1, source_target_pairs={{0,8},{8,16},{16,24},{24,32},{32,40},{40,48},{48,56},{56,64},{64,7... | collective-permute-start | bytes 1179656 | tf_op jit(solution)/shard_map/ppermute | solution.py:9
  123.4 16.1 %collective-permute-start.5 = (bf16[1024,192]{1,0:T(8,128)(2,1)S(1)}, bf16[1024,192]{1,0:T(8,128)(2,1)S(1)}, u32[]{:S(2)}, u32[]{:S(2)}) collective-permute-start(bf16[1024,192]{1,0:T(8,128)(2,1)S(1)} %collective-permute-done.4), channel_id=1, source_target_pairs={{0,8},{8,16},{16,24},{24,32},{32,40},{40,48},{48,56},{56,64},{64,7... | collective-permute-start | bytes 1179656 | tf_op jit(solution)/shard_map/ppermute | solution.py:9
  139.5 15.2 %collective-permute-start.6 = (bf16[1024,192]{1,0:T(8,128)(2,1)S(1)}, bf16[1024,192]{1,0:T(8,128)(2,1)S(1)}, u32[]{:S(2)}, u32[]{:S(2)}) collective-permute-start(bf16[1024,192]{1,0:T(8,128)(2,1)S(1)} %collective-permute-done.5), channel_id=1, source_target_pairs={{0,8},{8,16},{16,24},{24,32},{32,40},{40,48},{48,56},{56,64},{64,7... | collective-permute-start | bytes 1179656 | tf_op jit(solution)/shard_map/ppermute | solution.py:9
  154.7 14.1 %collective-permute-start.7 = (bf16[1024,192]{1,0:T(8,128)(2,1)S(1)}, bf16[1024,192]{1,0:T(8,128)(2,1)S(1)}, u32[]{:S(2)}, u32[]{:S(2)}) collective-permute-start(bf16[1024,192]{1,0:T(8,128)(2,1)S(1)} %collective-permute-done.6), channel_id=1, source_target_pairs={{0,8},{8,16},{16,24},{24,32},{32,40},{40,48},{48,56},{56,64},{64,7... | collective-permute-start | bytes 1179656 | tf_op jit(solution)/shard_map/ppermute | solution.py:9
  168.8 14.1 %collective-permute-start.8 = (bf16[1024,192]{1,0:T(8,128)(2,1)S(1)}, bf16[1024,192]{1,0:T(8,128)(2,1)S(1)}, u32[]{:S(2)}, u32[]{:S(2)}) collective-permute-start(bf16[1024,192]{1,0:T(8,128)(2,1)S(1)} %collective-permute-done.7), channel_id=1, source_target_pairs={{0,8},{8,16},{16,24},{24,32},{32,40},{40,48},{48,56},{56,64},{64,7... | collective-permute-start | bytes 1179656 | tf_op jit(solution)/shard_map/ppermute | solution.py:9
  182.9 14.1 %collective-permute-start.9 = (bf16[1024,192]{1,0:T(8,128)(2,1)S(1)}, bf16[1024,192]{1,0:T(8,128)(2,1)S(1)}, u32[]{:S(2)}, u32[]{:S(2)}) collective-permute-start(bf16[1024,192]{1,0:T(8,128)(2,1)S(1)} %collective-permute-done.8), channel_id=1, source_target_pairs={{0,8},{8,16},{16,24},{24,32},{32,40},{40,48},{48,56},{56,64},{64,7... | collective-permute-start | bytes 1179656 | tf_op jit(solution)/shard_map/ppermute | solution.py:9
Sparse Core Ops, SparseCore 0:
  199.8 92.2 all-reduce.1
where the time goes:
time: 301 us; the launch traced here: 300 us
  waiting for transfers between devices  243 us (81%)
  starting transfers between devices  25 us (8%)
  matrix products  14.1 us (5%)
  between operations  13.6 us (5%)
    ppermute x10, waiting for transfers between devices, shifted(): lax.ppermute(array, axis, [(i, (i + by) % count) for i in range(count)])  150 us
    psum x1, waiting for transfers between devices, local(): summed = lax.psum(total, 'layer')  92.4 us
    ppermute x10, starting transfers between devices, shifted(): lax.ppermute(array, axis, [(i, (i + by) % count) for i in range(count)])  25 us
    dot_general x8, matrix products, local(): total = total + jnp.dot(kernel, weights, preferred_element_type=jnp.float32)  14.1 us
  transfers between devices with their start and end apart: 11, of which 11 were waited for; matrix products, arithmetic and copies ran while one was open for 4% of the time, Pallas kernels for 0%

commit v1 on v0

v1 whole, which is shorter than its diff:
```python
import functools

import numpy as np

import jax
import jax.numpy as jnp
from jax import lax
from jax.experimental import pallas as pl
from jax.experimental.pallas import tpu as pltpu
from jax.sharding import PartitionSpec as P

MESH = pl.DeviceIdType.MESH
BF = jnp.bfloat16
F32 = jnp.float32

NX, NP, NZ, NK = 4, 2, 8, 4
ROWS, FEATS, RHS = 1024, 128, 64
HALF = ROWS // 2
LANES = 128
GROUPS = 8
PACK = HALF // GROUPS
WIDTH = LANES // GROUPS
TILES = HALF // LANES
MSG = HALF + TILES * RHS + PACK
DEPTH = 2 * FEATS
LOG2E = float(np.log2(np.e))


def pieces(value):
    first = value.astype(BF).astype(F32)
    rest = value - first
    second = rest.astype(BF).astype(F32)
    third = (rest - second).astype(BF).astype(F32)
    return first, second, third


def choose(index, values, others):
    result = others
    for at, value in values:
        result = jnp.where(index == at, value, result)
    return result


def kernel(scale, pts, dirs, out, rbuf, msg, cbuf, maug, acc, obuf, stage, fin, ybuf, send, recv):
    blk, layer = lax.axis_index("blk"), lax.axis_index("layer")
    x, p, z = blk % NX, (blk // NX) % NP, blk // (NX * NP)
    k, c = layer // 2, layer % 2
    near = jnp.where(k == 0, 0, jnp.where(k == 1, 1, jnp.where(k == 2, 7, 2)))

    def at(xx=x, pp=p, zz=z, kk=k, cc=c):
        return ((zz * NP + pp) * NX + xx, kk * 2 + cc)

    def along_x(by):
        return at(xx=lax.rem(x + by, NX))

    def along_z(by):
        return at(zz=lax.rem(z + by + 2 * NZ, NZ))

    def along_k(by):
        return at(kk=lax.rem(k + by, NK))

    mate = at(cc=1 - c)
    pair_near = at(pp=1 - p)
    pair_far = at(pp=1 - p, kk=lax.rem(k + 2 * p - 1 + NK, NK))

    barrier = pltpu.get_barrier_semaphore()

    def greet(device):
        pl.semaphore_signal(barrier, inc=1, device_id=device, device_id_type=MESH)

    for by in range(1, NX):
        greet(along_x(by))
    for by in range(1, NK):
        greet(along_k(by))
    greet(mate)
    greet(pair_near)
    greet(pair_far)
    greet(along_z(near + 4))

    @pl.when(k != 0)
    def _():
        greet(along_z(near))

    for h in range(NK):
        rows = pts[pl.ds(pl.multiple_of((2 * h + c) * LANES, LANES), LANES), :]
        turned = rows.astype(F32).T
        rbuf[0, 0:FEATS, h * LANES:(h + 1) * LANES] = turned.astype(BF)
        norm = -0.5 * jnp.sum(turned * turned, axis=0, keepdims=True)
        first, second, third = pieces(norm)
        row = lax.broadcasted_iota(jnp.int32, (WIDTH, LANES), 0)
        extra = choose(
            row, [(0, first), (1, second), (2, third)], jnp.where(row < 6, 1.0, 0.0)
        )
        rbuf[0, FEATS:FEATS + WIDTH, h * LANES:(h + 1) * LANES] = extra.astype(BF)

    lane = lax.broadcasted_iota(jnp.int32, (PACK, LANES), 1)
    packed = jnp.zeros((PACK, LANES), F32)
    for g in range(GROUPS):
        rows = pts[pl.ds(pl.multiple_of(c * HALF + g * PACK, PACK), PACK), :]
        msg[g * PACK:(g + 1) * PACK, :] = rows
        wide = rows.astype(F32)
        norm = -0.5 * jnp.sum(wide * wide, axis=1, keepdims=True)
        packed = jnp.where(lane // WIDTH == g, norm, packed)
    for t in range(TILES):
        cols = pl.ds(pl.multiple_of(c * HALF + t * LANES, LANES), LANES)
        msg[HALF + t * RHS:HALF + (t + 1) * RHS, :] = dirs[:, cols]
    first, second, third = pieces(packed)
    place = lane % WIDTH
    extra = choose(
        place, [(3, first), (4, second), (5, third)], jnp.where(place < 3, 1.0, 0.0)
    )
    msg[HALF + TILES * RHS:MSG, :] = extra.astype(BF)

    pl.semaphore_wait(barrier, jnp.where(k == 0, 10, 11))

    def copy(n, src, dst, device):
        return pltpu.make_async_remote_copy(
            src_ref=src,
            dst_ref=dst,
            send_sem=send.at[n],
            recv_sem=recv.at[n],
            device_id=device,
            device_id_type=MESH,
        )

    z_near = copy(0, msg, cbuf.at[0, 0], along_z(-near))
    z_far = copy(1, msg, cbuf.at[2, 0], along_z(-near - 4))
    own = pltpu.make_async_copy(msg, cbuf.at[0, 0], recv.at[0])
    y_near = copy(2, cbuf.at[0, 0], cbuf.at[1, 0], pair_near)
    y_far = copy(3, cbuf.at[2, 0], cbuf.at[3, 0], pair_far)
    shared = [copy(4 + s, cbuf.at[s, 0], cbuf.at[s, 1], mate) for s in range(4)]
    r_used = pl.ds(0, FEATS + WIDTH)
    rows_x = [
        copy(8 + by, rbuf.at[0, r_used], rbuf.at[by, r_used], along_x(by)) for by in range(1, NX)
    ]
    back_x = [
        copy(11 + by, stage.at[by - 1], obuf.at[by - 1], along_x(NX - by)) for by in range(1, NX)
    ]
    back_k = [
        copy(14 + by, fin.at[lax.rem(k + by, NK)], ybuf.at[by - 1], along_k(by))
        for by in range(1, NK)
    ]

    @pl.when(k != 0)
    def _():
        z_near.start()

    @pl.when(k == 0)
    def _():
        own.start()

    for by in (1, 3, 2):
        rows_x[by - 1].start()
    z_far.start()

    masks = [jnp.where(lane // WIDTH == g, 1.0, 0.0).astype(BF) for g in range(GROUPS)]

    def spread_norms(s, half):
        tile = cbuf[s, half, HALF + TILES * RHS:MSG, :]
        for g in range(GROUPS):
            maug[s, half * HALF + g * PACK:half * HALF + (g + 1) * PACK, :] = tile * masks[g]

    def spread_rows(by):
        tile = rbuf[by, FEATS:FEATS + WIDTH, :]
        for g in range(1, GROUPS):
            rbuf[by, FEATS + g * WIDTH:FEATS + (g + 1) * WIDTH, :] = tile

    def product(sources, by):
        left = jnp.concatenate(
            [
                jnp.concatenate([cbuf[s, half, 0:HALF, :] for s in sources for half in range(2)], axis=0),
                jnp.concatenate([maug[s] for s in sources], axis=0),
            ],
            axis=1,
        )
        weights = jnp.concatenate(
            [
                cbuf[s, half, HALF + t * RHS:HALF + (t + 1) * RHS, :]
                for s in sources
                for half in range(2)
                for t in range(TILES)
            ],
            axis=1,
        )
        power = jnp.dot(left, rbuf[by], preferred_element_type=F32)
        value = jnp.minimum(jnp.exp2(power * scale).astype(BF), jnp.ones((), BF))
        return jnp.dot(weights, value, preferred_element_type=F32)

    spread_rows(0)
    z_near.wait_recv()
    y_near.start()
    shared[0].start()
    spread_norms(0, 0)
    for by in (1, 3, 2):
        rows_x[by - 1].wait_recv()
        spread_rows(by)
    shared[0].wait_recv()
    spread_norms(0, 1)
    for by in range(NX):
        acc[by] = product((0,), by)

    y_near.wait_recv()
    shared[1].start()
    spread_norms(1, 0)
    z_far.wait_recv()
    y_far.start()
    shared[2].start()
    spread_norms(2, 0)
    shared[1].wait_recv()
    spread_norms(1, 1)
    for by in range(NX):
        acc[by] += product((1,), by)

    y_far.wait_recv()
    shared[3].start()
    spread_norms(3, 0)
    shared[2].wait_recv()
    spread_norms(2, 1)
    shared[3].wait_recv()
    spread_norms(3, 1)
    for by in (2, 1, 3):
        stage[by - 1] = (acc[by] + product((2, 3), by)).astype(BF)
        back_x[by - 1].start()
    total = acc[0] + product((2, 3), 0)
    for by in (2, 1, 3):
        back_x[by - 1].wait_recv()
        total += obuf[by - 1].astype(F32)
    for h in range(NK):
        fin[h] = total[:, h * LANES:(h + 1) * LANES]
    for by in range(1, NK):
        back_k[by - 1].start()
    result = fin[k]
    for by in range(1, NK):
        back_k[by - 1].wait_recv()
        result += ybuf[by - 1]
    out[...] = result

    @pl.when(k != 0)
    def _():
        z_near.wait_send()

    for one in (z_far, y_near, y_far, *shared, *rows_x, *back_x, *back_k):
        one.wait_send()


def local(points, directions):
    gamma = 0.5 / points.shape[1]
    turned = pl.pallas_call(
        functools.partial(kernel, 2.0 * gamma * LOG2E),
        out_shape=jax.ShapeDtypeStruct((RHS, LANES), F32),
        in_specs=[pl.BlockSpec(memory_space=pltpu.VMEM)] * 2,
        out_specs=pl.BlockSpec(memory_space=pltpu.VMEM),
        scratch_shapes=[
            pltpu.VMEM((NX, DEPTH, HALF), BF),
            pltpu.VMEM((MSG, LANES), BF),
            pltpu.VMEM((4, 2, MSG, LANES), BF),
            pltpu.VMEM((4, ROWS, LANES), BF),
            pltpu.VMEM((NX, RHS, HALF), F32),
            pltpu.VMEM((NX - 1, RHS, HALF), BF),
            pltpu.VMEM((NX - 1, RHS, HALF), BF),
            pltpu.VMEM((NK, RHS, LANES), F32),
            pltpu.VMEM((NK - 1, RHS, LANES), F32),
            pltpu.SemaphoreType.DMA((18,)),
            pltpu.SemaphoreType.DMA((18,)),
        ],
        compiler_params=pltpu.CompilerParams(
            collective_id=0, has_side_effects=True, vmem_limit_bytes=48 * 2**20
        ),
        name="gauss",
    )(points, directions.T)
    return turned.T


def solution(mesh):
    in_specs = (P("blk", None), P("blk", None))
    out_specs = P(("blk", "layer"), None)
    return jax.shard_map(local, mesh=mesh, in_specs=in_specs, out_specs=out_specs, check_vma=False)
```

time: 301 us -> 54.2 us (0.18)
  waiting for transfers between devices: 243 us -> 0 us
  Pallas kernels: 0 us -> 51.5 us
  starting transfers between devices: 25 us -> 0 us
  matrix products: 14.1 us -> 0 us
  between operations: 13.6 us -> 0.01 us
    ppermute x10 -> x0, waiting for transfers between devices: 150 us -> none  [shifted(): lax.ppermute(array, axis, [(i, (i + by) % count) for i in range(count)])]
    psum x1 -> x0, waiting for transfers between devices: 92.4 us -> none  [local(): summed = lax.psum(total, 'layer')]
    pallas_call x0 -> x1, Pallas kernels: none -> 51.5 us  [local(): pl.pallas_call(functools.partial(kernel, 2.0 * gamma * LOG2E), out_shape=...]
    ppermute x10 -> x0, starting transfers between devices: 25 us -> none  [shifted(): lax.ppermute(array, axis, [(i, (i + by) % count) for i in range(count)])]
    dot_general x8 -> x0, matrix products: 14.1 us -> none  [local(): total = total + jnp.dot(kernel, weights, preferred_element_type=jnp.float32)]
  transfers between devices with their start and end apart: 11 -> 0, of which waited for: 11 -> 0; matrix products, arithmetic and copies ran while one was open for 4% -> 0% of each run, Pallas kernels for 0% -> 0%
where the time goes in v1:
time: 54.2 us; the launch traced here: 54 us
  Pallas kernels  51.5 us (95%)
  local copies, waits for them, and re-layouts  2.47 us (5%)
    pallas_call x1, Pallas kernels, local(): pl.pallas_call(functools.partial(kernel, 2.0 * gamma * LOG2E), out_shape=...  51.5 us
    unnamed x5, local copies, waits for them, and re-layouts  2.47 us

profile of v1, /device:TPU:1, one launch (start us, length us, event | category | flops | bytes accessed | tf_op | source)
XLA Modules:
  0.0 54.0 jit_solution(161967066610243075)
XLA Ops:
  0.0 0.0 copy-start
  0.0 0.9 %copy-done = bf16[1024,128]{1,0:T(8,128)(2,1)S(1)} copy-done((bf16[1024,128]{1,0:T(8,128)(2,1)S(1)}, bf16[1024,128]{1,0:T(8,128)(2,1)}, u32[]{:S(2)}) %copy-start) | copy-done | bytes 262168
  1.0 0.0 copy-start.1
  1.0 0.9 %copy-done.1 = bf16[1024,64]{0,1:T(8,128)(2,1)S(1)} copy-done((bf16[1024,64]{0,1:T(8,128)(2,1)S(1)}, bf16[1024,64]{0,1:T(8,128)(2,1)}, u32[]{:S(2)}) %copy-start.1) | copy-done | bytes 131096
  1.9 51.5 %gauss.1 = f32[64,128]{1,0:T(8,128)S(1)} custom-call(bf16[1024,128]{1,0:T(8,128)(2,1)S(1)} %copy-done, bf16[64,1024]{1,0:T(8,128)(2,1)S(1)} %bitcast.2), custom_call_target="tpu_custom_call" | custom-call | tf_op jit(solution)/shard_map/gauss/pallas_call | solution.py:248
  53.4 0.6 %copy.4 = f32[128,64]{0,1:T(8,128)} copy(f32[128,64]{0,1:T(8,128)S(1)} %bitcast.3) | data formatting | bytes 65536
Async XLA Ops:
  0.0 0.9 %copy-start = (bf16[1024,128]{1,0:T(8,128)(2,1)S(1)}, bf16[1024,128]{1,0:T(8,128)(2,1)}, u32[]{:S(2)}) copy-start(bf16[1024,128]{1,0:T(8,128)(2,1)} %pts.1) | copy-start | bytes 786436
  1.0 0.9 %copy-start.1 = (bf16[1024,64]{0,1:T(8,128)(2,1)S(1)}, bf16[1024,64]{0,1:T(8,128)(2,1)}, u32[]{:S(2)}) copy-start(bf16[1024,64]{0,1:T(8,128)(2,1)} %param.3) | copy-start | bytes 393220

commit v2 on v1

v2 whole, which is shorter than its diff:
```python
import functools

import numpy as np

import jax
import jax.numpy as jnp
from jax import lax
from jax.experimental import pallas as pl
from jax.experimental.pallas import tpu as pltpu
from jax.sharding import PartitionSpec as P

MESH = pl.DeviceIdType.MESH
BF = jnp.bfloat16
F32 = jnp.float32

NX, NP, NZ, NK = 4, 2, 8, 4
ROWS, FEATS, RHS = 1024, 128, 64
HALF = ROWS // 2
LANES = 128
PARTS = 2
PART = HALF // PARTS
GROUPS = 8
PACK = PART // GROUPS
WIDTH = LANES // GROUPS
TILES = PART // LANES
NORMS = PART + TILES * RHS
MSG = NORMS + PACK
DEPTH = 2 * FEATS
LOG2E = float(np.log2(np.e))


def pieces(value):
    first = value.astype(BF).astype(F32)
    rest = value - first
    second = rest.astype(BF).astype(F32)
    third = (rest - second).astype(BF).astype(F32)
    return first, second, third


def choose(index, values, others):
    result = others
    for at, value in values:
        result = jnp.where(index == at, value, result)
    return result


def kernel(scale, pts_hbm, dirs_hbm, out, pts, dirs, msg, rbuf, cbuf, maug, acc, stage, obuf, fin, ybuf, load, send, recv):
    blk, layer = lax.axis_index("blk"), lax.axis_index("layer")
    x, p, z = blk % NX, (blk // NX) % NP, blk // (NX * NP)
    k, c = layer // 2, layer % 2
    turn = jnp.where((k == 1) | (k == 2), c, 0)
    near = choose(k, [(0, 0), (1, 1 + 6 * turn), (2, 7 - 6 * turn)], 2)

    def at(xx=x, pp=p, zz=z, kk=k, cc=c):
        return ((zz * NP + pp) * NX + xx, kk * 2 + cc)

    def along_x(by):
        return at(xx=(x + by) % NX)

    def along_z(by):
        return at(zz=(z + by + 2 * NZ) % NZ)

    def along_k(by):
        return at(kk=(k + by) % NK)

    mate = at(cc=1 - c)
    pair_k = (k + c * (2 * p - 1) + NK) % NK

    def across(by):
        return at(xx=(x + by) % NX, pp=1 - p, kk=pair_k)

    barrier = pltpu.get_barrier_semaphore()

    def greet(device):
        pl.semaphore_signal(barrier, inc=1, device_id=device, device_id_type=MESH)

    greet(along_z(near + 4))

    @pl.when(k != 0)
    def _():
        greet(along_z(near))

    for by in range(1, NK):
        greet(along_k(by))
    for by in range(1, NX):
        greet(along_x(by))
    for by in range(NX):
        greet(across(by))
    greet(mate)

    load_pts = pltpu.make_async_copy(pts_hbm, pts, load.at[0])
    load_dirs = pltpu.make_async_copy(dirs_hbm, dirs, load.at[1])
    load_pts.start()
    load_dirs.start()
    load_pts.wait()

    row = lax.broadcasted_iota(jnp.int32, (WIDTH, LANES), 0)
    for h in range(NK):
        rows = pts[pl.ds(pl.multiple_of((2 * h + c) * LANES, LANES), LANES), :]
        turned = rows.astype(F32).T
        rbuf[0, 0:FEATS, h * LANES:(h + 1) * LANES] = turned.astype(BF)
        norm = -0.5 * jnp.sum(turned * turned, axis=0, keepdims=True)
        first, second, third = pieces(norm)
        extra = choose(
            row, [(0, first), (1, second), (2, third)], jnp.where(row < 6, 1.0, 0.0)
        ).astype(BF)
        for g in range(GROUPS):
            rbuf[0, FEATS + g * WIDTH:FEATS + (g + 1) * WIDTH, h * LANES:(h + 1) * LANES] = extra

    load_dirs.wait()
    lane = lax.broadcasted_iota(jnp.int32, (PACK, LANES), 1)
    place = lane % WIDTH
    for q in range(PARTS):
        packed = jnp.zeros((PACK, LANES), F32)
        for g in range(GROUPS):
            start = pl.multiple_of(c * HALF + q * PART + g * PACK, PACK)
            rows = pts[pl.ds(start, PACK), :]
            msg[q, g * PACK:(g + 1) * PACK, :] = rows
            wide = rows.astype(F32)
            norm = -0.5 * jnp.sum(wide * wide, axis=1, keepdims=True)
            packed = jnp.where(lane // WIDTH == g, norm, packed)
        for t in range(TILES):
            cols = pl.ds(pl.multiple_of(c * HALF + q * PART + t * LANES, LANES), LANES)
            msg[q, PART + t * RHS:PART + (t + 1) * RHS, :] = dirs[:, cols]
        first, second, third = pieces(packed)
        extra = choose(
            place, [(3, first), (4, second), (5, third)], jnp.where(place < 3, 1.0, 0.0)
        )
        msg[q, NORMS:MSG, :] = extra.astype(BF)

    pl.semaphore_wait(barrier, jnp.where(k == 0, 12, 13))

    def copy(n, src, dst, device):
        return pltpu.make_async_remote_copy(
            src_ref=src,
            dst_ref=dst,
            send_sem=send.at[n],
            recv_sem=recv.at[n],
            device_id=device,
            device_id_type=MESH,
        )

    parts = range(PARTS)
    z_near = [copy(q, msg.at[q], cbuf.at[0, 0, q], along_z(-near)) for q in parts]
    z_own = [pltpu.make_async_copy(msg.at[q], cbuf.at[0, 0, q], recv.at[q]) for q in parts]
    z_far = [copy(4 + q, msg.at[q], cbuf.at[1, 0, q], along_z(-near - 4)) for q in parts]
    shared = [
        [copy(8 + 4 * n + q, cbuf.at[n, 0, q], cbuf.at[n, 1, q], mate) for q in parts]
        for n in range(2)
    ]
    r_used = pl.ds(0, FEATS + WIDTH)
    rows_x = [
        copy(15 + by, rbuf.at[0, r_used], rbuf.at[by, r_used], along_x(by)) for by in range(1, NX)
    ]
    rows_y = [
        copy(19 + by, rbuf.at[by, r_used], rbuf.at[NX + by, r_used], across(0)) for by in range(NX)
    ]
    back_x = {
        by: copy(23 + by, stage.at[by], obuf.at[by], along_x(NX - by) if by < NX else across(2 * NX - by))
        for by in range(1, 2 * NX)
    }
    back_k = [
        copy(30 + by, fin.at[(k + by) % NK], ybuf.at[by - 1], along_k(by)) for by in range(1, NK)
    ]

    @pl.when(k != 0)
    def _():
        for one in z_near:
            one.start()

    @pl.when(k == 0)
    def _():
        for one in z_own:
            one.start()

    for by in (1, 3, 2):
        rows_x[by - 1].start()
    rows_y[0].start()
    for one in z_far:
        one.start()

    masks = [jnp.where(lane // WIDTH == g, 1.0, 0.0).astype(BF) for g in range(GROUPS)]

    def spread_norms(n, half):
        for q in parts:
            tile = cbuf[n, half, q, NORMS:MSG, :]
            for g in range(GROUPS):
                first = half * HALF + q * PART + g * PACK
                maug[n, first:first + PACK, :] = tile * masks[g]

    def pass_on(n, arrives, leave):
        for q in parts:
            arrives[q].wait_recv()
            for one in leave:
                one[q].start()
        spread_norms(n, 0)

    def from_mate(n):
        for one in shared[n]:
            one.wait_recv()
        spread_norms(n, 1)

    def spread_rows(by):
        tile = rbuf[by, FEATS:FEATS + WIDTH, :]
        for g in range(1, GROUPS):
            rbuf[by, FEATS + g * WIDTH:FEATS + (g + 1) * WIDTH, :] = tile

    def product(sources, by):
        pieces_of = [(n, half, q) for n in sources for half in range(2) for q in parts]
        lhs = jnp.concatenate(
            [
                jnp.concatenate([cbuf[n, half, q, 0:PART, :] for n, half, q in pieces_of], axis=0),
                jnp.concatenate([maug[n] for n in sources], axis=0),
            ],
            axis=1,
        )
        weights = jnp.concatenate(
            [
                cbuf[n, half, q, PART + t * RHS:PART + (t + 1) * RHS, :]
                for n, half, q in pieces_of
                for t in range(TILES)
            ],
            axis=1,
        )
        power = jnp.dot(lhs, rbuf[by], preferred_element_type=F32)
        value = jnp.minimum(jnp.exp2(power * scale).astype(BF), jnp.ones((), BF))
        return jnp.dot(weights, value, preferred_element_type=F32)

    for by in (1, 3, 2):
        rows_x[by - 1].wait_recv()
        rows_y[by].start()
        spread_rows(by)
    pass_on(0, z_near, (shared[0],))
    from_mate(0)
    for by in range(NX):
        acc[by] = product((0,), by)

    for by in range(NX):
        rows_y[by].wait_recv()
        spread_rows(NX + by)
    pass_on(1, z_far, (shared[1],))
    for by in range(NX, 2 * NX):
        acc[by] = product((0,), by)

    from_mate(1)
    for group in ((6, 2), (5, 1), (7, 3), (4,)):
        for by in group:
            stage[by] = (acc[by] + product((1,), by)).astype(BF)
        for by in group:
            back_x[by].start()
    total = acc[0] + product((1,), 0)
    for by in (6, 2, 5, 1, 7, 3, 4):
        back_x[by].wait_recv()
        total += obuf[by].astype(F32)
    for h in range(NK):
        fin[h] = total[:, h * LANES:(h + 1) * LANES].astype(BF)
        acc[0, :, h * LANES:(h + 1) * LANES] = total[:, h * LANES:(h + 1) * LANES]
    for by in (2, 1, 3):
        back_k[by - 1].start()
    result = acc[0, :, pl.ds(pl.multiple_of(k * LANES, LANES), LANES)]
    for by in (1, 3, 2):
        back_k[by - 1].wait_recv()
        result += ybuf[by - 1].astype(F32)
    out[...] = result

    @pl.when(k != 0)
    def _():
        for one in z_near:
            one.wait_send()

    groups = (z_far, *shared, rows_x, rows_y, back_x.values(), back_k)
    for group in groups:
        for one in group:
            one.wait_send()


def local(points, directions):
    gamma = 0.5 / points.shape[1]
    turned = pl.pallas_call(
        functools.partial(kernel, 2.0 * gamma * LOG2E),
        out_shape=jax.ShapeDtypeStruct((RHS, LANES), F32),
        in_specs=[pl.BlockSpec(memory_space=pl.ANY)] * 2,
        out_specs=pl.BlockSpec(memory_space=pltpu.VMEM),
        scratch_shapes=[
            pltpu.VMEM((ROWS, FEATS), BF),
            pltpu.VMEM((RHS, ROWS), BF),
            pltpu.VMEM((PARTS, MSG, LANES), BF),
            pltpu.VMEM((2 * NX, DEPTH, HALF), BF),
            pltpu.VMEM((2, 2, PARTS, MSG, LANES), BF),
            pltpu.VMEM((2, ROWS, LANES), BF),
            pltpu.VMEM((2 * NX, RHS, HALF), F32),
            pltpu.VMEM((2 * NX, RHS, HALF), BF),
            pltpu.VMEM((2 * NX, RHS, HALF), BF),
            pltpu.VMEM((NK, RHS, LANES), BF),
            pltpu.VMEM((NK - 1, RHS, LANES), BF),
            pltpu.SemaphoreType.DMA((2,)),
            pltpu.SemaphoreType.DMA((34,)),
            pltpu.SemaphoreType.DMA((34,)),
        ],
        compiler_params=pltpu.CompilerParams(
            collective_id=0, has_side_effects=True, vmem_limit_bytes=60 * 2**20
        ),
        name="gauss",
    )(points, directions.T)
    return turned.T


def solution(mesh):
    in_specs = (P("blk", None), P("blk", None))
    out_specs = P(("blk", "layer"), None)
    return jax.shard_map(local, mesh=mesh, in_specs=in_specs, out_specs=out_specs, check_vma=False)
```

time: 54.2 us -> 46.7 us (0.86)
  Pallas kernels: 51.5 us -> 45.2 us
  local copies, waits for them, and re-layouts: 2.47 us -> 1.38 us
    pallas_call x1, Pallas kernels: 51.5 us -> 45.2 us  [local(): pl.pallas_call(functools.partial(kernel, 2.0 * gamma * LOG2E), out_shape=...]
    unnamed x5 -> x1, local copies, waits for them, and re-layouts: 2.47 us -> 1.38 us
where the time goes in v2:
time: 46.7 us; the launch traced here: 46.6 us
  Pallas kernels  45.2 us (97%)
  local copies, waits for them, and re-layouts  1.38 us (3%)
    pallas_call x1, Pallas kernels, local(): pl.pallas_call(functools.partial(kernel, 2.0 * gamma * LOG2E), out_shape=...  45.2 us
    unnamed x1, local copies, waits for them, and re-layouts  1.38 us

profile of v2, /device:TPU:1, one launch (start us, length us, event | category | flops | bytes accessed | tf_op | source)
XLA Modules:
  0.0 46.6 jit_solution(10215079860715514398)
XLA Ops:
  0.0 45.2 %gauss.1 = f32[64,128]{1,0:T(8,128)} custom-call(bf16[1024,128]{1,0:T(8,128)(2,1)} %pts_hbm.1, bf16[64,1024]{1,0:T(8,128)(2,1)} %bitcast.2), custom_call_target="tpu_custom_call" | custom-call | tf_op jit(solution)/shard_map/gauss/pallas_call | solution.py:279
  45.2 1.4 %copy.4 = f32[128,64]{0,1:T(8,128)} copy(f32[128,64]{0,1:T(8,128)} %bitcast.3) | data formatting | bytes 65536

commit v3 on v2

--- a/solution.py
+++ b/solution.py
@@ -17,8 +17,8 @@
 ROWS, FEATS, RHS = 1024, 128, 64
 HALF = ROWS // 2
 LANES = 128
-PARTS = 2
-PART = HALF // PARTS
+QUARTER = ROWS // NK
+PART = QUARTER // 2
 GROUPS = 8
 PACK = PART // GROUPS
 WIDTH = LANES // GROUPS
@@ -44,12 +44,10 @@
     return result
 
 
-def kernel(scale, pts_hbm, dirs_hbm, out, pts, dirs, msg, rbuf, cbuf, maug, acc, stage, obuf, fin, ybuf, load, send, recv):
+def kernel(scale, pts_hbm, dirs_hbm, out, pts, dirs, rbuf, cbuf, maug, acc, stage, obuf, fin, ybuf, load, send, recv):
     blk, layer = lax.axis_index("blk"), lax.axis_index("layer")
     x, p, z = blk % NX, (blk // NX) % NP, blk // (NX * NP)
     k, c = layer // 2, layer % 2
-    turn = jnp.where((k == 1) | (k == 2), c, 0)
-    near = choose(k, [(0, 0), (1, 1 + 6 * turn), (2, 7 - 6 * turn)], 2)
 
     def at(xx=x, pp=p, zz=z, kk=k, cc=c):
         return ((zz * NP + pp) * NX + xx, kk * 2 + cc)
@@ -74,12 +72,8 @@
     def greet(device):
         pl.semaphore_signal(barrier, inc=1, device_id=device, device_id_type=MESH)
 
-    greet(along_z(near + 4))
-
-    @pl.when(k != 0)
-    def _():
-        greet(along_z(near))
-
+    for by in (2, -2, 1, -1):
+        greet(along_z(by))
     for by in range(1, NK):
         greet(along_k(by))
     for by in range(1, NX):
@@ -110,25 +104,23 @@
     load_dirs.wait()
     lane = lax.broadcasted_iota(jnp.int32, (PACK, LANES), 1)
     place = lane % WIDTH
-    for q in range(PARTS):
+    for half in range(2):
+        base = k * QUARTER + lax.rem(c + half, 2) * PART
         packed = jnp.zeros((PACK, LANES), F32)
         for g in range(GROUPS):
-            start = pl.multiple_of(c * HALF + q * PART + g * PACK, PACK)
-            rows = pts[pl.ds(start, PACK), :]
-            msg[q, g * PACK:(g + 1) * PACK, :] = rows
+            rows = pts[pl.ds(pl.multiple_of(base + g * PACK, PACK), PACK), :]
+            cbuf[0, half, g * PACK:(g + 1) * PACK, :] = rows
             wide = rows.astype(F32)
             norm = -0.5 * jnp.sum(wide * wide, axis=1, keepdims=True)
             packed = jnp.where(lane // WIDTH == g, norm, packed)
-        for t in range(TILES):
-            cols = pl.ds(pl.multiple_of(c * HALF + q * PART + t * LANES, LANES), LANES)
-            msg[q, PART + t * RHS:PART + (t + 1) * RHS, :] = dirs[:, cols]
+        cbuf[0, half, PART:NORMS, :] = dirs[:, pl.ds(pl.multiple_of(base, LANES), LANES)]
         first, second, third = pieces(packed)
         extra = choose(
             place, [(3, first), (4, second), (5, third)], jnp.where(place < 3, 1.0, 0.0)
         )
-        msg[q, NORMS:MSG, :] = extra.astype(BF)
-
-    pl.semaphore_wait(barrier, jnp.where(k == 0, 12, 13))
+        cbuf[0, half, NORMS:MSG, :] = extra.astype(BF)
+
+    pl.semaphore_wait(barrier, 15)
 
     def copy(n, src, dst, device):
         return pltpu.make_async_remote_copy(
@@ -140,14 +132,11 @@
             device_id_type=MESH,
         )
 
-    parts = range(PARTS)
-    z_near = [copy(q, msg.at[q], cbuf.at[0, 0, q], along_z(-near)) for q in parts]
-    z_own = [pltpu.make_async_copy(msg.at[q], cbuf.at[0, 0, q], recv.at[q]) for q in parts]
-    z_far = [copy(4 + q, msg.at[q], cbuf.at[1, 0, q], along_z(-near - 4)) for q in parts]
-    shared = [
-        [copy(8 + 4 * n + q, cbuf.at[n, 0, q], cbuf.at[n, 1, q], mate) for q in parts]
-        for n in range(2)
-    ]
+    along = {by: copy(by, cbuf.at[0, 0], cbuf.at[by, 0], along_z(-by)) for by in (1, 2, 6, 7)}
+    along[3] = copy(3, cbuf.at[2, 0], cbuf.at[3, 0], along_z(-1))
+    along[5] = copy(5, cbuf.at[6, 0], cbuf.at[5, 0], along_z(1))
+    along[4] = copy(4, cbuf.at[6 - 4 * c, 0], cbuf.at[4, 0], along_z(2 - 4 * c))
+    shared = {by: copy(7 + by, cbuf.at[by, 0], cbuf.at[by, 1], mate) for by in range(1, NZ)}
     r_used = pl.ds(0, FEATS + WIDTH)
     rows_x = [
         copy(15 + by, rbuf.at[0, r_used], rbuf.at[by, r_used], along_x(by)) for by in range(1, NX)
@@ -163,42 +152,35 @@
         copy(30 + by, fin.at[(k + by) % NK], ybuf.at[by - 1], along_k(by)) for by in range(1, NK)
     ]
 
-    @pl.when(k != 0)
-    def _():
-        for one in z_near:
-            one.start()
-
-    @pl.when(k == 0)
-    def _():
-        for one in z_own:
-            one.start()
-
-    for by in (1, 3, 2):
+    for by in (2, 6, 1, 7):
+        along[by].start()
+    for by in (1, 3):
         rows_x[by - 1].start()
     rows_y[0].start()
-    for one in z_far:
-        one.start()
+    rows_x[1].start()
 
     masks = [jnp.where(lane // WIDTH == g, 1.0, 0.0).astype(BF) for g in range(GROUPS)]
 
-    def spread_norms(n, half):
-        for q in parts:
-            tile = cbuf[n, half, q, NORMS:MSG, :]
-            for g in range(GROUPS):
-                first = half * HALF + q * PART + g * PACK
-                maug[n, first:first + PACK, :] = tile * masks[g]
-
-    def pass_on(n, arrives, leave):
-        for q in parts:
-            arrives[q].wait_recv()
-            for one in leave:
-                one[q].start()
-        spread_norms(n, 0)
-
-    def from_mate(n):
-        for one in shared[n]:
-            one.wait_recv()
-        spread_norms(n, 1)
+    def spread_norms(by, half):
+        tile = cbuf[by, half, NORMS:MSG, :]
+        for g in range(GROUPS):
+            first = half * PART + g * PACK
+            maug[by, first:first + PACK, :] = tile * masks[g]
+
+    def pass_on(offsets, onward):
+        for by in offsets:
+            along[by].wait_recv()
+        for by in onward:
+            along[by].start()
+        for by in offsets:
+            shared[by].start()
+        for by in offsets:
+            spread_norms(by, 0)
+
+    def from_mate(*offsets):
+        for by in offsets:
+            shared[by].wait_recv()
+            spread_norms(by, 1)
 
     def spread_rows(by):
         tile = rbuf[by, FEATS:FEATS + WIDTH, :]
@@ -206,50 +188,63 @@
             rbuf[by, FEATS + g * WIDTH:FEATS + (g + 1) * WIDTH, :] = tile
 
     def product(sources, by):
-        pieces_of = [(n, half, q) for n in sources for half in range(2) for q in parts]
+        halves = [(n, half) for n in sources for half in range(2)]
         lhs = jnp.concatenate(
             [
-                jnp.concatenate([cbuf[n, half, q, 0:PART, :] for n, half, q in pieces_of], axis=0),
+                jnp.concatenate([cbuf[n, half, 0:PART, :] for n, half in halves], axis=0),
                 jnp.concatenate([maug[n] for n in sources], axis=0),
             ],
             axis=1,
         )
-        weights = jnp.concatenate(
-            [
-                cbuf[n, half, q, PART + t * RHS:PART + (t + 1) * RHS, :]
-                for n, half, q in pieces_of
-                for t in range(TILES)
-            ],
-            axis=1,
-        )
+        weights = jnp.concatenate([cbuf[n, half, PART:NORMS, :] for n, half in halves], axis=1)
         power = jnp.dot(lhs, rbuf[by], preferred_element_type=F32)
         value = jnp.minimum(jnp.exp2(power * scale).astype(BF), jnp.ones((), BF))
         return jnp.dot(weights, value, preferred_element_type=F32)
 
-    for by in (1, 3, 2):
+    spread_norms(0, 0)
+    spread_norms(0, 1)
+    pass_on((1, 7), ())
+    for by in (1, 3):
         rows_x[by - 1].wait_recv()
         rows_y[by].start()
         spread_rows(by)
-    pass_on(0, z_near, (shared[0],))
-    from_mate(0)
-    for by in range(NX):
-        acc[by] = product((0,), by)
-
-    for by in range(NX):
+    pass_on((2, 6), (3, 5, 4))
+    rows_y[0].wait_recv()
+    spread_rows(4)
+    from_mate(1, 7, 2, 6)
+    close = (0, 1, 7, 2, 6)
+    for by in (1, 3, 4):
+        acc[by] = product(close, by)
+
+    rows_x[1].wait_recv()
+    rows_y[2].start()
+    spread_rows(2)
+    acc[2] = product(close, 2)
+    for by in (1, 3):
         rows_y[by].wait_recv()
         spread_rows(NX + by)
-    pass_on(1, z_far, (shared[1],))
-    for by in range(NX, 2 * NX):
-        acc[by] = product((0,), by)
-
-    from_mate(1)
-    for group in ((6, 2), (5, 1), (7, 3), (4,)):
+    for by in (5, 7):
+        acc[by] = product(close, by)
+
+    pass_on((3, 5, 4), ())
+    from_mate(3, 5, 4)
+    rest = (3, 5, 4)
+
+    def give(*group):
         for by in group:
-            stage[by] = (acc[by] + product((1,), by)).astype(BF)
+            value = product(close + rest, by) if by == 6 else acc[by] + product(rest, by)
+            stage[by] = value.astype(BF)
         for by in group:
             back_x[by].start()
-    total = acc[0] + product((1,), 0)
-    for by in (6, 2, 5, 1, 7, 3, 4):
+
+    give(5, 2)
+    rows_y[2].wait_recv()
+    spread_rows(6)
+    give(6)
+    give(1, 7)
+    give(3, 4)
+    total = product(close + rest, 0)
+    for by in (5, 2, 6, 1, 7, 3, 4):
         back_x[by].wait_recv()
         total += obuf[by].astype(F32)
     for h in range(NK):
@@ -263,12 +258,7 @@
         result += ybuf[by - 1].astype(F32)
     out[...] = result
 
-    @pl.when(k != 0)
-    def _():
-        for one in z_near:
-            one.wait_send()
-
-    groups = (z_far, *shared, rows_x, rows_y, back_x.values(), back_k)
+    groups = (along.values(), shared.values(), rows_x, rows_y, back_x.values(), back_k)
     for group in groups:
         for one in group:
             one.wait_send()
@@ -284,10 +274,9 @@
         scratch_shapes=[
             pltpu.VMEM((ROWS, FEATS), BF),
             pltpu.VMEM((RHS, ROWS), BF),
-            pltpu.VMEM((PARTS, MSG, LANES), BF),
             pltpu.VMEM((2 * NX, DEPTH, HALF), BF),
-            pltpu.VMEM((2, 2, PARTS, MSG, LANES), BF),
-            pltpu.VMEM((2, ROWS, LANES), BF),
+            pltpu.VMEM((NZ, 2, MSG, LANES), BF),
+            pltpu.VMEM((NZ, QUARTER, LANES), BF),
             pltpu.VMEM((2 * NX, RHS, HALF), F32),
             pltpu.VMEM((2 * NX, RHS, HALF), BF),
             pltpu.VMEM((2 * NX, RHS, HALF), BF),

time: 46.7 us -> 44.5 us (0.953)
  Pallas kernels: 45.2 us -> 42.8 us
    pallas_call x1, Pallas kernels: 45.2 us -> 42.8 us  [local(): pl.pallas_call(functools.partial(kernel, 2.0 * gamma * LOG2E), out_shape=...]
where the time goes in v3:
time: 44.5 us; the launch traced here: 44.2 us
  Pallas kernels  42.8 us (96%)
  local copies, waits for them, and re-layouts  1.38 us (3%)
    pallas_call x1, Pallas kernels, local(): pl.pallas_call(functools.partial(kernel, 2.0 * gamma * LOG2E), out_shape=...  42.8 us
    unnamed x1, local copies, waits for them, and re-layouts  1.38 us

profile of v3, /device:TPU:1, one launch (start us, length us, event | category | flops | bytes accessed | tf_op | source)
XLA Modules:
  0.0 44.2 jit_solution(9505254610426588550)
XLA Ops:
  0.0 42.8 %gauss.1 = f32[64,128]{1,0:T(8,128)} custom-call(bf16[1024,128]{1,0:T(8,128)(2,1)} %pts_hbm.1, bf16[64,1024]{1,0:T(8,128)(2,1)} %bitcast.2), custom_call_target="tpu_custom_call" | custom-call | tf_op jit(solution)/shard_map/gauss/pallas_call | solution.py:269
  42.9 1.4 %copy.4 = f32[128,64]{0,1:T(8,128)} copy(f32[128,64]{0,1:T(8,128)} %bitcast.3) | data formatting | bytes 65536

commit v4 on v3

--- a/solution.py
+++ b/solution.py
@@ -67,6 +67,11 @@
     def across(by):
         return at(xx=(x + by) % NX, pp=1 - p, kk=pair_k)
 
+    load_pts = pltpu.make_async_copy(pts_hbm, pts, load.at[0])
+    load_dirs = pltpu.make_async_copy(dirs_hbm, dirs, load.at[1])
+    load_pts.start()
+    load_dirs.start()
+
     barrier = pltpu.get_barrier_semaphore()
 
     def greet(device):
@@ -82,10 +87,6 @@
         greet(across(by))
     greet(mate)
 
-    load_pts = pltpu.make_async_copy(pts_hbm, pts, load.at[0])
-    load_dirs = pltpu.make_async_copy(dirs_hbm, dirs, load.at[1])
-    load_pts.start()
-    load_dirs.start()
     load_pts.wait()
 
     row = lax.broadcasted_iota(jnp.int32, (WIDTH, LANES), 0)
@@ -211,22 +212,26 @@
     pass_on((2, 6), (3, 5, 4))
     rows_y[0].wait_recv()
     spread_rows(4)
-    from_mate(1, 7, 2, 6)
-    close = (0, 1, 7, 2, 6)
+    from_mate(1, 7)
     for by in (1, 3, 4):
-        acc[by] = product(close, by)
+        acc[by] = product((0, 1, 7), by)
 
     rows_x[1].wait_recv()
     rows_y[2].start()
     spread_rows(2)
+    from_mate(2, 6)
+    for by in (1, 3, 4):
+        acc[by] += product((2, 6), by)
+    close = (0, 1, 7, 2, 6)
     acc[2] = product(close, 2)
-    for by in (1, 3):
-        rows_y[by].wait_recv()
-        spread_rows(NX + by)
-    for by in (5, 7):
-        acc[by] = product(close, by)
-
+
+    rows_y[1].wait_recv()
+    spread_rows(5)
+    acc[5] = product(close, 5)
     pass_on((3, 5, 4), ())
+    rows_y[3].wait_recv()
+    spread_rows(7)
+    acc[7] = product(close, 7)
     from_mate(3, 5, 4)
     rest = (3, 5, 4)
 
@@ -238,11 +243,12 @@
             back_x[by].start()
 
     give(5, 2)
+    give(7, 1)
     rows_y[2].wait_recv()
     spread_rows(6)
     give(6)
-    give(1, 7)
-    give(3, 4)
+    give(3)
+    give(4)
     total = product(close + rest, 0)
     for by in (5, 2, 6, 1, 7, 3, 4):
         back_x[by].wait_recv()

time: 44.5 us -> 43.6 us (0.980)
  Pallas kernels: 42.8 us -> 42 us
    pallas_call x1, Pallas kernels: 42.8 us -> 42 us  [local(): pl.pallas_call(functools.partial(kernel, 2.0 * gamma * LOG2E), out_shape=...]
where the time goes in v4:
time: 43.6 us; the launch traced here: 43.4 us
  Pallas kernels  42 us (96%)
  local copies, waits for them, and re-layouts  1.38 us (3%)
    pallas_call x1, Pallas kernels, local(): pl.pallas_call(functools.partial(kernel, 2.0 * gamma * LOG2E), out_shape=...  42 us
    unnamed x1, local copies, waits for them, and re-layouts  1.38 us

profile of v4, /device:TPU:1, one launch (start us, length us, event | category | flops | bytes accessed | tf_op | source)
XLA Modules:
  0.0 43.4 jit_solution(1656727263895688872)
XLA Ops:
  0.0 42.0 %gauss.1 = f32[64,128]{1,0:T(8,128)} custom-call(bf16[1024,128]{1,0:T(8,128)(2,1)} %pts_hbm.1, bf16[64,1024]{1,0:T(8,128)(2,1)} %bitcast.2), custom_call_target="tpu_custom_call" | custom-call | tf_op jit(solution)/shard_map/gauss/pallas_call | solution.py:275
  42.0 1.4 %copy.4 = f32[128,64]{0,1:T(8,128)} copy(f32[128,64]{0,1:T(8,128)} %bitcast.3) | data formatting | bytes 65536

commit v5 on v4

--- a/solution.py
+++ b/solution.py
@@ -101,25 +101,6 @@
         ).astype(BF)
         for g in range(GROUPS):
             rbuf[0, FEATS + g * WIDTH:FEATS + (g + 1) * WIDTH, h * LANES:(h + 1) * LANES] = extra
-
-    load_dirs.wait()
-    lane = lax.broadcasted_iota(jnp.int32, (PACK, LANES), 1)
-    place = lane % WIDTH
-    for half in range(2):
-        base = k * QUARTER + lax.rem(c + half, 2) * PART
-        packed = jnp.zeros((PACK, LANES), F32)
-        for g in range(GROUPS):
-            rows = pts[pl.ds(pl.multiple_of(base + g * PACK, PACK), PACK), :]
-            cbuf[0, half, g * PACK:(g + 1) * PACK, :] = rows
-            wide = rows.astype(F32)
-            norm = -0.5 * jnp.sum(wide * wide, axis=1, keepdims=True)
-            packed = jnp.where(lane // WIDTH == g, norm, packed)
-        cbuf[0, half, PART:NORMS, :] = dirs[:, pl.ds(pl.multiple_of(base, LANES), LANES)]
-        first, second, third = pieces(packed)
-        extra = choose(
-            place, [(3, first), (4, second), (5, third)], jnp.where(place < 3, 1.0, 0.0)
-        )
-        cbuf[0, half, NORMS:MSG, :] = extra.astype(BF)
 
     pl.semaphore_wait(barrier, 15)
 
@@ -153,11 +134,31 @@
         copy(30 + by, fin.at[(k + by) % NK], ybuf.at[by - 1], along_k(by)) for by in range(1, NK)
     ]
 
-    for by in (2, 6, 1, 7):
-        along[by].start()
     for by in (1, 3):
         rows_x[by - 1].start()
     rows_y[0].start()
+
+    load_dirs.wait()
+    lane = lax.broadcasted_iota(jnp.int32, (PACK, LANES), 1)
+    place = lane % WIDTH
+    for half in range(2):
+        base = k * QUARTER + lax.rem(c + half, 2) * PART
+        packed = jnp.zeros((PACK, LANES), F32)
+        for g in range(GROUPS):
+            rows = pts[pl.ds(pl.multiple_of(base + g * PACK, PACK), PACK), :]
+            cbuf[0, half, g * PACK:(g + 1) * PACK, :] = rows
+            wide = rows.astype(F32)
+            norm = -0.5 * jnp.sum(wide * wide, axis=1, keepdims=True)
+            packed = jnp.where(lane // WIDTH == g, norm, packed)
+        cbuf[0, half, PART:NORMS, :] = dirs[:, pl.ds(pl.multiple_of(base, LANES), LANES)]
+        first, second, third = pieces(packed)
+        extra = choose(
+            place, [(3, first), (4, second), (5, third)], jnp.where(place < 3, 1.0, 0.0)
+        )
+        cbuf[0, half, NORMS:MSG, :] = extra.astype(BF)
+
+    for by in (1, 7, 2, 6):
+        along[by].start()
     rows_x[1].start()
 
     masks = [jnp.where(lane // WIDTH == g, 1.0, 0.0).astype(BF) for g in range(GROUPS)]

time: 43.6 us -> 43.2 us (level)
  no operation moved by 1% of the time
where the time goes in v5:
time: 43.2 us; the launch traced here: 43 us
  Pallas kernels  41.6 us (96%)
  local copies, waits for them, and re-layouts  1.38 us (3%)
    pallas_call x1, Pallas kernels, local(): pl.pallas_call(functools.partial(kernel, 2.0 * gamma * LOG2E), out_shape=...  41.6 us
    unnamed x1, local copies, waits for them, and re-layouts  1.38 us

profile of v5, /device:TPU:1, one launch (start us, length us, event | category | flops | bytes accessed | tf_op | source)
XLA Modules:
  0.0 43.0 jit_solution(9652441757115691032)
XLA Ops:
  0.0 41.6 %gauss.1 = f32[64,128]{1,0:T(8,128)} custom-call(bf16[1024,128]{1,0:T(8,128)(2,1)} %pts_hbm.1, bf16[64,1024]{1,0:T(8,128)(2,1)} %bitcast.2), custom_call_target="tpu_custom_call" | custom-call | tf_op jit(solution)/shard_map/gauss/pallas_call | solution.py:276
  41.6 1.4 %copy.4 = f32[128,64]{0,1:T(8,128)} copy(f32[128,64]{0,1:T(8,128)} %bitcast.3) | data formatting | bytes 65536

commit v6 on v5

--- a/solution.py
+++ b/solution.py
@@ -77,14 +77,14 @@
     def greet(device):
         pl.semaphore_signal(barrier, inc=1, device_id=device, device_id_type=MESH)
 
+    for by in (2, 1, 3):
+        greet(along_k(by))
+        greet(across(by))
     for by in (2, -2, 1, -1):
         greet(along_z(by))
-    for by in range(1, NK):
-        greet(along_k(by))
-    for by in range(1, NX):
+    for by in (2, 1, 3):
         greet(along_x(by))
-    for by in range(NX):
-        greet(across(by))
+    greet(across(0))
     greet(mate)
 
     load_pts.wait()

time: 43.2 us -> 42.9 us (level)
  no operation moved by 1% of the time
where the time goes in v6:
time: 42.9 us; the launch traced here: 42.7 us
  Pallas kernels  41.3 us (96%)
  local copies, waits for them, and re-layouts  1.38 us (3%)
    pallas_call x1, Pallas kernels, local(): pl.pallas_call(functools.partial(kernel, 2.0 * gamma * LOG2E), out_shape=...  41.3 us
    unnamed x1, local copies, waits for them, and re-layouts  1.38 us

profile of v6, /device:TPU:1, one launch (start us, length us, event | category | flops | bytes accessed | tf_op | source)
XLA Modules:
  0.0 42.7 jit_solution(12054602660112777401)
XLA Ops:
  0.0 41.3 %gauss.1 = f32[64,128]{1,0:T(8,128)} custom-call(bf16[1024,128]{1,0:T(8,128)(2,1)} %pts_hbm.1, bf16[64,1024]{1,0:T(8,128)(2,1)} %bitcast.2), custom_call_target="tpu_custom_call" | custom-call | tf_op jit(solution)/shard_map/gauss/pallas_call | solution.py:276
  41.3 1.4 %copy.4 = f32[128,64]{0,1:T(8,128)} copy(f32[128,64]{0,1:T(8,128)} %bitcast.3) | data formatting | bytes 65536
